TPU v7x, 128 devices: a whole 4x4x4 slice. The times are simulated.
128 devices in a mesh: space: 8 (over z, y_lo), vel: 16 (over y_hi, x, core).
Axes of the slice: x: 4, y: 4 (y_hi: 2, y_lo: 2; y = y_hi * 2 + y_lo), z: 4, core: 2. Of those that a mesh axis runs over, the one named last changes fastest.
Arguments:
- distribution: bfloat16 [4096, 48, 8, 128], P('vel', 'space'), may hold values from -6 to 6
- up_factor: bfloat16 [4096, 256], P('vel'), may hold values from -0.75 to 0.75
- down_factor: bfloat16 [4096, 256], P('vel'), may hold values from -0.09375 to 0.09375
- decay: float32 [4096], P('vel'), may hold values from 0.3 to 3
- wall_kind: int32 [2, 8, 128], replicated, may hold values from 0 to 2
Outputs:
- advanced: bfloat16 [4096, 48, 8, 128], P('vel', 'space')
Inputs may be any that keep to these rules, and one draw needn't show every extreme that they name: `wall_kind`: 0 marks a diffuse wall at rest, 1 a diffuse heated wall, 2 an open face.
All inputs are finite; a program needn't handle non-finite values.
Results may differ from a plain program's by a relative error of at most 0.0046.
Values may be sent and summed in bfloat16 or wider, within the bound.
A program may use at most 192 MiB of HBM per device.

v0:
```python
import jax
import jax.numpy as jnp
from jax import lax
from jax.sharding import PartitionSpec as P

NV = 16
STEPS = 2


speed_range = 8.0
time_ratio = 0.08
wall_heat = 3.0


def with_halo(block, sides, width):
    for axis, dim in sides:
        count = lax.axis_size(axis)
        forward = [(i, i + 1) for i in range(count - 1)]
        backward = [(target, source) for source, target in forward]
        low = lax.ppermute(
            lax.slice_in_dim(block, block.shape[dim] - width, None, axis=dim), axis, forward
        )
        high = lax.ppermute(lax.slice_in_dim(block, 0, width, axis=dim), axis, backward)
        block = jnp.concatenate([low, block, high], axis=dim)
    return block


def components(vel_ids):
    spacing = speed_range / NV
    midpoint = (NV - 1) / 2.0
    along_z = ((vel_ids // (NV * NV)).astype(jnp.float32) - midpoint) * spacing
    along_x = ((vel_ids // NV % NV).astype(jnp.float32) - midpoint) * spacing
    along_y = ((vel_ids % NV).astype(jnp.float32) - midpoint) * spacing
    return (along_z, along_x, along_y)


def wall_ghost(outflux, kind_face, maxwell, energy, norm):
    sigma = outflux / norm
    heating = jnp.where(kind_face == 1, wall_heat, 0.0)
    opened = jnp.where(kind_face == 2, 0.0, 1.0)
    return (
        maxwell[:, None, None]
        * (sigma[None] + heating[None] * energy[:, None, None])
        * opened[None]
    )


def transport(centre, lower_plane, upper_plane, along_z, along_x, along_y):
    dimensions = centre.ndim
    shaped = (-1,) + (1,) * (dimensions - 1)
    axis_x = dimensions - 2
    axis_y = dimensions - 1
    plus_z = jnp.maximum(along_z, 0.0).reshape(shaped)
    minus_z = jnp.minimum(along_z, 0.0).reshape(shaped)
    plus_x = jnp.maximum(along_x, 0.0).reshape(shaped)
    minus_x = jnp.minimum(along_x, 0.0).reshape(shaped)
    plus_y = jnp.maximum(along_y, 0.0).reshape(shaped)
    minus_y = jnp.minimum(along_y, 0.0).reshape(shaped)
    result = plus_z * (centre - lower_plane) + minus_z * (upper_plane - centre)
    result = (
        result
        + plus_x * (centre - jnp.roll(centre, 1, axis_x))
        + minus_x * (jnp.roll(centre, -1, axis_x) - centre)
    )
    result = (
        result
        + plus_y * (centre - jnp.roll(centre, 1, axis_y))
        + minus_y * (jnp.roll(centre, -1, axis_y) - centre)
    )
    return result


def body(distribution, up_factor, down_factor, decay, wall_kind):
    local_vel, depth, width_x, width_y = distribution.shape
    cells = depth * width_x * width_y
    vel_ids = lax.axis_index("vel") * local_vel + jnp.arange(local_vel, dtype=jnp.int32)
    along_z, along_x, along_y = components(vel_ids)
    speed_sq = along_z * along_z + along_x * along_x + along_y * along_y
    maxwell = jnp.exp(-0.5 * speed_sq)
    energy = 0.5 * speed_sq - 1.5
    all_ids = jnp.arange(NV**3, dtype=jnp.int32)
    full_z, full_x, full_y = components(all_ids)
    norm = jnp.sum(
        jnp.maximum(full_z, 0.0)
        * jnp.exp(-0.5 * (full_z * full_z + full_x * full_x + full_y * full_y))
    )
    slab = lax.axis_index("space")
    slabs = lax.axis_size("space")
    current = distribution
    for step in range(STEPS):
        low_face = current[:, 0].astype(jnp.float32)
        high_face = current[:, depth - 1].astype(jnp.float32)
        out_low = jnp.sum(jnp.maximum(-along_z, 0.0)[:, None, None] * low_face, axis=0)
        out_high = jnp.sum(jnp.maximum(along_z, 0.0)[:, None, None] * high_face, axis=0)
        outflux = lax.psum(jnp.stack([out_low, out_high]), "vel")
        ghost_low = wall_ghost(outflux[0], wall_kind[0], maxwell, energy, norm)
        ghost_high = wall_ghost(outflux[1], wall_kind[1], maxwell, energy, norm)
        padded = with_halo(current, (("space", 1),), 1)
        first_plane = jnp.where(slab == 0, ghost_low, padded[:, 0].astype(jnp.float32))
        last_plane = jnp.where(
            slab == slabs - 1, ghost_high, padded[:, depth + 1].astype(jnp.float32)
        )
        lower_plane = jnp.concatenate(
            [first_plane[:, None], padded[:, 1:depth].astype(jnp.float32)], axis=1
        )
        upper_plane = jnp.concatenate(
            [padded[:, 2 : depth + 1].astype(jnp.float32), last_plane[:, None]], axis=1
        )
        centre = current.astype(jnp.float32)
        moved = transport(centre, lower_plane, upper_plane, along_z, along_x, along_y)
        flat_rows = current.reshape(local_vel, cells)
        coeffs = lax.psum_scatter(
            lax.dot_general(
                flat_rows, down_factor, (((0,), (0,)), ((), ())), preferred_element_type=jnp.float32
            ),
            "vel",
            scatter_dimension=0,
            tiled=True,
        ).astype(jnp.bfloat16)
        gained = lax.dot_general(
            up_factor,
            lax.all_gather(coeffs, "vel", axis=0, tiled=True),
            (((1,), (1,)), ((), ())),
            preferred_element_type=jnp.float32,
        ).reshape(current.shape)
        updated = (
            centre
            - time_ratio * moved
            + time_ratio * (gained - decay[:, None, None, None] * centre)
        )
        current = updated.astype(jnp.bfloat16)
    return current


def solution(mesh):
    return jax.shard_map(
        body,
        mesh=mesh,
        in_specs=(P("vel", "space", None, None), P("vel", None), P("vel", None), P("vel"), P()),
        out_specs=P("vel", "space", None, None),
        check_vma=False,
    )
```

profile of v0, /device:TPU:1, one launch (start us, length us, event | category | flops | bytes accessed | tf_op | source)
XLA Modules:
  0.0 418.3 jit_solution(15023858921832519522)
XLA Ops:
  6.5 0.9 copy-done
  7.4 5.9 %fusion.35 = f32[6144,256]{1,0:T(8,128)} fusion(bf16[256,256]{1,0:T(8,128)(2,1)S(1)} %copy-done, bf16[32,8,48,128]{3,2,1,0:T(8,128)(2,1)} %bitcast.76), kind=kOutput, calls=%fused_computation.51 | convolution fusion | flops 805306368 | bytes 9568256 | tf_op jit(solution)/shard_map/dot_general | solution.py:113
  13.3 0.0 reduce-scatter.3.cloned.1.call-update
  13.3 0.0 all-gather.3.cloned.1.call-start
  13.4 91.6 %reduce-scatter.3.cloned.1.call-done = f32[384,256]{1,0:T(8,128)} async-done(((f32[6144,256]{1,0:T(8,128)}), f32[384,256]{1,0:T(8,128)}) %reduce-scatter.3.cloned.1.call-update) | async-done | bytes 393232 | tf_op jit(solution)/shard_map/reduce_scatter | solution.py:112
  105.0 1.7 convert_element_type.151
  106.7 0.0 all-gather.3.cloned.1.call-update
  106.7 0.0 reduce-scatter.5.cloned.1.call-start
  106.8 1.1 slice_bitcast_fusion.2
  107.9 3.0 collective-permute-start
  110.9 1.3 collective-permute-start.1
  112.2 0.7 fusion.86
  112.9 1.0 fusion.57
  113.9 35.5 %psum.14 = f32[2,8,128]{2,1,0:T(8,128)S(1)} all-reduce(f32[2,8,128]{2,1,0:T(8,128)S(1)} %pad_maximum_fusion), channel_id=1, replica_groups=mesh['space'=8,'vel'=16] {'vel'}, use_global_device_ids=true, to_apply=%region_2.3 | all-reduce | flops 2048 | bytes 16384 | tf_op jit(solution)/shard_map/psum | solution.py:95
  149.5 4.7 %slice_convert_fusion.3 = (f32[256,5,8,128]{3,2,1,0:T(8,128)}, f32[256,5,8,128]{3,2,1,0:T(8,128)}) fusion(bf16[256,6,8,128]{3,2,1,0:T(8,128)(2,1)S(1)} %copy-done.2), kind=kLoop, calls=%fused_computation.57 | loop fusion | flops 2621440 | bytes 15728640 | tf_op jit(solution)/shard_map/convert_element_type | solution.py:104
  154.2 2.1 fusion.103
  156.3 5.5 %fusion.106 = (f32[256,6,8,127]{3,2,1,0:T(8,128)}, f32[256,6,8,127]{3,2,1,0:T(8,128)}) fusion(bf16[256,6,8,128]{3,2,1,0:T(8,128)(2,1)S(1)} %copy-done.2), kind=kLoop, calls=%fused_computation.182 | loop fusion | bytes 24969216 | tf_op jit(solution)/shard_map/jit(_roll_static)/slice | solution.py:67
  161.8 5.5 %fusion.105 = (f32[256,6,8,1]{3,2,1,0:T(8,128)}, f32[256,6,8,1]{3,2,1,0:T(8,128)}) fusion(bf16[256,6,8,128]{3,2,1,0:T(8,128)(2,1)S(1)} %copy-done.2), kind=kLoop, calls=%fused_computation.181 | loop fusion | bytes 196608 | tf_op jit(solution)/shard_map/jit(_roll_static)/slice | solution.py:67
  167.3 5.4 %fusion.104 = (f32[256,6,7,128]{3,2,1,0:T(8,128)}, f32[256,6,7,128]{3,2,1,0:T(8,128)}) fusion(bf16[256,6,8,128]{3,2,1,0:T(8,128)(2,1)S(1)} %copy-done.2), kind=kLoop, calls=%fused_computation.180 | loop fusion | bytes 22020096 | tf_op jit(solution)/shard_map/jit(_roll_static)/slice | solution.py:62
  172.7 0.6 fusion.90
  173.4 2.6 fusion.41
  176.0 0.0 collective-permute-done.1
  176.0 2.6 fusion.49
  178.7 5.5 %fusion.107 = f32[6144,256]{1,0:T(8,128)} fusion(bf16[6144,256]{1,0:T(8,128)(2,1)} %all-gather.3.cloned.1.call-done, bf16[256,256]{1,0:T(8,128)(2,1)S(1)} %copy-done.3), kind=kOutput, calls=%fused_computation.183 | convolution fusion | flops 805306368 | bytes 9568256 | tf_op jit(solution)/shard_map/dot_general | solution.py:120
  184.2 6.7 %copy.10 = f32[256,6,8,128]{3,2,1,0:T(8,128)} copy(f32[256,6,8,128]{0,3,2,1:T(8,128)} %bitcast.77) | data formatting | bytes 12582912 | tf_op jit(solution)/shard_map/reshape | solution.py:125
  190.9 21.8 %fusion.31 = bf16[256,6,8,128]{3,2,1,0:T(8,128)(2,1)S(1)} fusion(f32[256,6,8,128]{3,2,1,0:T(8,128)} %copy.10, f32[256,6,8,1]{3,2,1,0:T(8,128)} %get-tuple-element.30, f32[256,6,8,127]{3,2,1,0:T(8,128)} %get-tuple-element.32, f32[256,6,8,127]{3,2,1,0:T(8,128)} %get-tuple-element.31, f32[256,6,8,1]{3,2,1,0:T(8,128)} %get-tuple-element.29, ...), kind=kLoop, calls=%fused_computation.47 | loop fusion | flops 48758784 | bytes 50338816 | tf_op jit(solution)/shard_map/convert_element_type | solution.py:131
  212.6 4.0 fusion.32
  216.6 0.0 reduce-scatter.5.cloned.1.call-update
  216.6 0.0 all-gather.5.cloned.1.call-start
  216.7 89.4 %reduce-scatter.5.cloned.1.call-done = f32[384,256]{1,0:T(8,128)} async-done(((f32[6144,256]{1,0:T(8,128)}), f32[384,256]{1,0:T(8,128)}) %reduce-scatter.5.cloned.1.call-update) | async-done | bytes 393232 | tf_op jit(solution)/shard_map/reduce_scatter | solution.py:112
  306.1 1.7 convert_element_type.162
  307.8 0.0 all-gather.5.cloned.1.call-update
  307.8 1.0 slice_bitcast_fusion
  308.9 3.0 collective-permute-start.2
  311.9 1.3 collective-permute-start.3
  313.2 1.0 fusion.55
  314.2 35.5 %psum.15 = f32[2,8,128]{2,1,0:T(8,128)S(1)} all-reduce(f32[2,8,128]{2,1,0:T(8,128)S(1)} %pad_maximum_fusion.1), channel_id=1, replica_groups=mesh['space'=8,'vel'=16] {'vel'}, use_global_device_ids=true, to_apply=%region_7.8 | all-reduce | flops 2048 | bytes 16384 | tf_op jit(solution)/shard_map/psum | solution.py:95
  349.7 0.6 fusion.88
  350.3 2.1 fusion.99
  352.4 5.5 %fusion.102 = (f32[256,6,8,127]{3,2,1,0:T(8,128)}, f32[256,6,8,127]{3,2,1,0:T(8,128)}) fusion(bf16[256,6,8,128]{3,2,1,0:T(8,128)(2,1)S(1)} %fusion.31), kind=kLoop, calls=%fused_computation.178 | loop fusion | bytes 24969216 | tf_op jit(solution)/shard_map/jit(_roll_static)/slice | solution.py:67
  358.0 5.5 %fusion.100 = (f32[256,6,7,128]{3,2,1,0:T(8,128)}, f32[256,6,7,128]{3,2,1,0:T(8,128)}) fusion(bf16[256,6,8,128]{3,2,1,0:T(8,128)(2,1)S(1)} %fusion.31), kind=kLoop, calls=%fused_computation.176 | loop fusion | bytes 22020096 | tf_op jit(solution)/shard_map/jit(_roll_static)/slice | solution.py:62
  363.4 5.5 %fusion.101 = (f32[256,6,8,1]{3,2,1,0:T(8,128)}, f32[256,6,8,1]{3,2,1,0:T(8,128)}) fusion(bf16[256,6,8,128]{3,2,1,0:T(8,128)(2,1)S(1)} %fusion.31), kind=kLoop, calls=%fused_computation.177 | loop fusion | bytes 196608 | tf_op jit(solution)/shard_map/jit(_roll_static)/slice | solution.py:67
  368.9 4.7 %slice_convert_fusion.1 = (f32[256,5,8,128]{3,2,1,0:T(8,128)}, f32[256,5,8,128]{3,2,1,0:T(8,128)}) fusion(bf16[256,6,8,128]{3,2,1,0:T(8,128)(2,1)S(1)} %fusion.31), kind=kLoop, calls=%fused_computation.55 | loop fusion | flops 2621440 | bytes 15728640 | tf_op jit(solution)/shard_map/convert_element_type | solution.py:104
  373.6 0.0 collective-permute-done.2
  373.6 3.6 fusion.45
  377.2 5.5 %fusion.108 = f32[6144,256]{1,0:T(8,128)} fusion(bf16[6144,256]{1,0:T(8,128)(2,1)} %all-gather.5.cloned.1.call-done, bf16[256,256]{1,0:T(8,128)(2,1)S(1)} %copy-done.3), kind=kOutput, calls=%fused_computation.184 | convolution fusion | flops 805306368 | bytes 9568256 | tf_op jit(solution)/shard_map/dot_general | solution.py:120
  382.7 6.7 %copy.15 = f32[256,6,8,128]{3,2,1,0:T(8,128)} copy(f32[256,6,8,128]{0,3,2,1:T(8,128)} %bitcast.78) | data formatting | bytes 12582912 | tf_op jit(solution)/shard_map/reshape | solution.py:125
  389.4 22.4 %fusion.30 = bf16[256,6,8,128]{3,2,1,0:T(8,128)(2,1)} fusion(f32[256,6,8,128]{3,2,1,0:T(8,128)} %copy.15, f32[256,6,8,1]{3,2,1,0:T(8,128)} %get-tuple-element.18, f32[256,6,8,127]{3,2,1,0:T(8,128)} %get-tuple-element.20, f32[256,6,8,127]{3,2,1,0:T(8,128)} %get-tuple-element.19, f32[256,6,8,1]{3,2,1,0:T(8,128)} %get-tuple-element.17, ...), kind=kLoop, calls=%fused_computation.46 | loop fusion | flops 48758784 | bytes 50338816 | tf_op jit(solution)/shard_map/convert_element_type | solution.py:131
  (24 shorter events, 0.1 us)
Async XLA Ops:
  6.5 0.9 copy-start
  6.5 98.5 %reduce-scatter.3.cloned.1.call-start = ((), (), s32[]{:S(2)}) async-start(), calls=%async_computation.2 | async-start | bytes 6684672 | tf_op jit(solution)/shard_map/reduce_scatter | solution.py:112
  13.3 93.5 %copy-start.2 = (bf16[256,6,8,128]{3,2,1,0:T(8,128)(2,1)S(1)}, bf16[256,6,8,128]{3,2,1,0:T(8,128)(2,1)}, u32[]{:S(2)}) copy-start(bf16[256,6,8,128]{3,2,1,0:T(8,128)(2,1)} %param.5) | copy-start | bytes 9437188
  13.3 165.3 %all-gather.3.cloned.1.call-start = ((), (), s32[]{:S(2)}) async-start(), calls=%async_computation.3 | async-start | bytes 3342336 | tf_op jit(solution)/shard_map/all_gather | solution.py:122
  106.7 199.4 %reduce-scatter.5.cloned.1.call-start = ((), (), s32[]{:S(2)}) async-start(), calls=%async_computation.4 | async-start | bytes 6684672 | tf_op jit(solution)/shard_map/reduce_scatter | solution.py:112
  107.9 65.6 %collective-permute-start = (bf16[256,1,8,128]{3,2,0,1:T(8,128)(2,1)}, bf16[256,1,8,128]{3,2,0,1:T(8,128)(2,1)}, u32[]{:S(2)}, u32[]{:S(2)}) collective-permute-start(bf16[256,1,8,128]{3,2,0,1:T(8,128)(2,1)} %get-tuple-element.21), channel_id=1, source_target_pairs={{0,16},{16,32},{32,48},{48,64},{64,80},{80,96},{96,112},{1,17},{17... | collective-permute-start | bytes 1572872 | tf_op jit(solution)/shard_map/ppermute | solution.py:20
  110.9 65.1 %collective-permute-start.1 = (bf16[256,1,8,128]{3,2,1,0:T(8,128)(2,1)}, bf16[256,1,8,128]{3,2,1,0:T(8,128)(2,1)}, u32[]{:S(2)}, u32[]{:S(2)}) collective-permute-start(bf16[256,1,8,128]{3,2,1,0:T(8,128)(2,1)} %get-tuple-element.22), channel_id=1, source_target_pairs={{16,0},{32,16},{48,32},{64,48},{80,64},{96,80},{112,96},{17,1},{33... | collective-permute-start | bytes 1572872 | tf_op jit(solution)/shard_map/ppermute | solution.py:23
  167.3 6.1 %copy-start.4 = (s32[2,8,128]{2,1,0:T(8,128)S(1)}, s32[2,8,128]{2,1,0:T(8,128)}, u32[]{:S(2)}) copy-start(s32[2,8,128]{2,1,0:T(8,128)} %param.9) | copy-start | bytes 24580
  167.3 11.4 %copy-start.3 = (bf16[256,256]{1,0:T(8,128)(2,1)S(1)}, bf16[256,256]{1,0:T(8,128)(2,1)}, u32[]{:S(2)}) copy-start(bf16[256,256]{1,0:T(8,128)(2,1)} %param.6) | copy-start | bytes 393220
  184.2 6.7 %copy-start.5 = (f32[256]{0:T(256)S(1)}, f32[256]{0:T(256)}, u32[]{:S(2)}) copy-start(f32[256]{0:T(256)} %param.8) | copy-start | bytes 3076
  216.6 160.6 %all-gather.5.cloned.1.call-start = ((), (), s32[]{:S(2)}) async-start(), calls=%async_computation.5 | async-start | bytes 3342336 | tf_op jit(solution)/shard_map/all_gather | solution.py:122
  308.9 64.7 %collective-permute-start.2 = (bf16[256,1,8,128]{3,2,0,1:T(8,128)(2,1)}, bf16[256,1,8,128]{3,2,0,1:T(8,128)(2,1)}, u32[]{:S(2)}, u32[]{:S(2)}) collective-permute-start(bf16[256,1,8,128]{3,2,0,1:T(8,128)(2,1)} %get-tuple-element.9), channel_id=1, source_target_pairs={{0,16},{16,32},{32,48},{48,64},{64,80},{80,96},{96,112},{1,17},{17... | collective-permute-start | bytes 1572872 | tf_op jit(solution)/shard_map/ppermute | solution.py:20
  311.9 61.7 %collective-permute-start.3 = (bf16[256,1,8,128]{3,2,0,1:T(8,128)(2,1)}, bf16[256,1,8,128]{3,2,0,1:T(8,128)(2,1)}, u32[]{:S(2)}, u32[]{:S(2)}) collective-permute-start(bf16[256,1,8,128]{3,2,0,1:T(8,128)(2,1)} %get-tuple-element.10), channel_id=1, source_target_pairs={{16,0},{32,16},{48,32},{64,48},{80,64},{96,80},{112,96},{17,1},{33... | collective-permute-start | bytes 1572872 | tf_op jit(solution)/shard_map/ppermute | solution.py:23
  389.4 22.4 %copy-start.1 = (bf16[256,256]{1,0:T(8,128)(2,1)S(1)}, bf16[256,256]{1,0:T(8,128)(2,1)}, u32[]{:S(2)}) copy-start(bf16[256,256]{1,0:T(8,128)(2,1)} %param.7) | copy-start | bytes 393220
Sparse Core Ops, SparseCore 0:
  13.5 91.5 reduce-scatter.2
  107.5 54.3 all-gather.2
  216.8 89.3 reduce-scatter.4
  308.4 54.3 all-gather.4
where the time goes:
time: 420 us; the launch traced here: 418 us
  waiting for transfers between devices  181 us (43%)
  blocking collectives  71.1 us (17%)
  other arithmetic  69.8 us (17%)
  local copies, waits for them, and re-layouts  53.4 us (13%)
  matrix products  20.8 us (5%)
  between operations  13.3 us (3%)
  starting transfers between devices  8.72 us (2%)
    reduce_scatter x2, waiting for transfers between devices, body(): lax.psum_scatter(lax.dot_general(flat_rows, down_factor, (((0,), (0,)), (...  181 us
    psum x2, blocking collectives, body(): outflux = lax.psum(jnp.stack([out_low, out_high]), 'vel')  71.1 us
    convert_element_type x2, other arithmetic, body(): current = updated.astype(jnp.bfloat16)  44.2 us
    slice x4, local copies, waits for them, and re-layouts, transport(): jnp.roll(centre, 1, axis_y)  22 us
    slice x4, local copies, waits for them, and re-layouts, transport(): jnp.roll(centre, 1, axis_x)  15.1 us
    reshape x2, local copies, waits for them, and re-layouts, body(): gained = lax.dot_general(up_factor, lax.all_gather(coeffs, 'vel', axis=0,...  13.4 us
    dot_general x2, matrix products, body(): lax.dot_general(up_factor, lax.all_gather(coeffs, 'vel', axis=0, tiled=Tr...  11 us
    dot_general x2, matrix products, body(): lax.dot_general(flat_rows, down_factor, (((0,), (0,)), ((), ())), preferr...  9.84 us
  transfers between devices with their start and end apart: 8, of which 2 were waited for; matrix products, arithmetic and copies ran while one was open for 15% of the time, Pallas kernels for 0%

commit v1 on v0

v1 whole, which is shorter than its diff:
```python
import functools

import jax
import jax.numpy as jnp
from jax import lax
from jax.experimental import pallas as pl
from jax.experimental.pallas import tpu as pltpu
from jax.sharding import PartitionSpec as P

NV = 16
STEPS = 2
MESH = pl.DeviceIdType.MESH

speed_range = 8.0
time_ratio = 0.08
wall_heat = 3.0

SPACING = speed_range / NV
MIDPOINT = (NV - 1) / 2.0
F32 = jnp.float32
BF16 = jnp.bfloat16

CORE_SUM, PASS_SUM, NEAR_SUM, LAST_SUM, PAIR_SUM, OUT_B, OUT_A, OUT_PASS, CORE_OUT = range(9)
STAGES = 8


def kernel(
    depth,
    slabs,
    dist_ref,
    up_ref,
    down_ref,
    decay_ref,
    wall_ref,
    out_ref,
    state,
    raw,
    down_t,
    keep,
    slope_x,
    slope_y,
    part,
    sum_core_out,
    sum_core_in,
    sum_a_out,
    sum_a_in,
    sum_b_out,
    sum_b_in,
    sum_y_out,
    sum_y_in,
    coeffs,
    flux_out,
    flux_in,
    send_sem,
    recv_sem,
    halo_send,
    halo_recv,
    flux_send,
    flux_recv,
    in_sem,
    out_sem,
):
    chunks = STEPS * depth
    slab = lax.axis_index("space")
    vel = lax.axis_index("vel")
    core = lax.rem(vel, 2)
    chip = lax.rem(vel // 2, 4)
    upper = vel // 8
    sign = 2 * upper - 1
    flip = chip + 1 - 2 * lax.rem(chip, 2)
    mirror = 3 - chip
    chip_a = flip * (1 - core) + mirror * core
    chip_b = mirror * (1 - core) + flip * core
    chip_o = lax.rem(chip + 2, 4)

    def device(pair, x, c):
        return (slab, pair * 8 + x * 2 + c)

    to_core = device(upper, chip, 1 - core)
    to_a = device(upper, chip_a, core)
    to_b = device(upper, chip_b, core)
    to_pair = device(1 - upper, chip, core)
    to_slab = (slab + sign, vel)
    last = depth - 1
    source_plane = last * upper
    target_plane = last * (1 - upper)
    halo_slot = (depth + 1) * (1 - upper)
    sends_halo = slab != (slabs - 1) * upper
    takes_halo = slab != (slabs - 1) * (1 - upper)

    def level_of(q):
        return lax.rem(depth - lax.rem(q, depth), depth)

    def load(z):
        return pltpu.make_async_copy(dist_ref.at[:, z], raw.at[z], in_sem.at[z])

    def store(z):
        return pltpu.make_async_copy(raw.at[z], out_ref.at[:, z], out_sem.at[z])

    def remote(kind, q, src, dst, target):
        return pltpu.make_async_remote_copy(
            src_ref=src,
            dst_ref=dst,
            send_sem=send_sem.at[kind, q],
            recv_sem=recv_sem.at[kind, q],
            device_id=target,
            device_id_type=MESH,
        )

    mine = core * 4

    def message(kind, q):
        if kind == CORE_SUM:
            return remote(kind, q, sum_core_out.at[q], sum_core_in.at[q], to_core)
        if kind == PASS_SUM:
            return remote(kind, q, sum_a_out.at[q, 0], sum_a_in.at[q, 0], to_a)
        if kind == NEAR_SUM:
            return remote(kind, q, sum_a_out.at[q, 1], sum_a_in.at[q, 1], to_a)
        if kind == LAST_SUM:
            return remote(kind, q, sum_b_out.at[q], sum_b_in.at[q], to_b)
        if kind == PAIR_SUM:
            return remote(kind, q, sum_y_out.at[q], sum_y_in.at[q], to_pair)
        if kind == OUT_B:
            row = coeffs.at[q, mine + chip]
            return remote(kind, q, row, row, to_b)
        if kind == OUT_A:
            row = coeffs.at[q, mine + chip]
            return remote(kind, q, row, row, to_a)
        if kind == OUT_PASS:
            row = coeffs.at[q, mine + chip_b]
            return remote(kind, q, row, row, to_a)
        rows = coeffs.at[q, pl.ds(mine, 4)]
        return remote(kind, q, rows, rows, to_core)

    def halo(n):
        return pltpu.make_async_remote_copy(
            src_ref=state.at[n, 1 + source_plane],
            dst_ref=state.at[n, halo_slot],
            send_sem=halo_send.at[n],
            recv_sem=halo_recv.at[n],
            device_id=to_slab,
            device_id_type=MESH,
        )

    def flux(n, k):
        return pltpu.make_async_remote_copy(
            src_ref=flux_out.at[n],
            dst_ref=flux_in.at[n, chip * 2 + core],
            send_sem=flux_send.at[n, k],
            recv_sem=flux_recv.at[n, chip * 2 + core],
            device_id=(slab, (1 - upper) * 8 + k),
            device_id_type=MESH,
        )

    def flux_arrival(n, k):
        return pltpu.make_async_remote_copy(
            src_ref=flux_out.at[n],
            dst_ref=flux_in.at[n, k],
            send_sem=flux_send.at[n, k],
            recv_sem=flux_recv.at[n, k],
            device_id=(slab, (1 - upper) * 8 + k),
            device_id_type=MESH,
        )

    for z in range(depth):
        load((depth - z) % depth).start()

    barrier = pltpu.get_barrier_semaphore()

    def greet(target):
        pl.semaphore_signal(barrier, inc=1, device_id=target, device_id_type=MESH)

    for target in (to_core, to_a, to_b):
        greet(target)
    for k in range(8):
        greet((slab, (1 - upper) * 8 + k))

    greet((lax.rem(slab + slabs - 1, slabs), vel))
    greet((lax.rem(slab + 1, slabs), vel))

    ids = lax.broadcasted_iota(jnp.int32, (256, 128), 0)
    speed_x = jnp.abs(((ids >> 4).astype(F32) - MIDPOINT) * SPACING)
    speed_y = jnp.abs(((ids & 15).astype(F32) - MIDPOINT) * SPACING)
    speed_z = jnp.abs((vel.astype(F32) - MIDPOINT) * SPACING)
    decay = jnp.concatenate(
        [jnp.broadcast_to(decay_ref[i : i + 1, :], (128, 128)).T for i in range(2)], axis=0
    )
    keep[...] = 1.0 - time_ratio * (speed_x + speed_y + speed_z + decay)
    slope_x[...] = time_ratio * speed_x
    slope_y[...] = time_ratio * speed_y
    slope_z = time_ratio * speed_z
    down_t[...] = down_ref[...].T

    pl.semaphore_wait(barrier, 13)

    def project(n, z, x):
        pair = jnp.concatenate([state[n, 1 + z, x], state[n, 1 + z, x + 1]], axis=1)
        return jnp.dot(down_t[...], pair, preferred_element_type=F32)

    def begin(q):
        n, z = q // depth, level_of(q)

        @pl.when(q < depth)
        def _():
            load(z).wait()

            def block(i, carry):
                rows = pl.ds(pl.multiple_of(i * 16, 16), 16)
                state[0, 1 + z, :, rows, :] = jnp.swapaxes(raw[z, rows], 0, 1)
                return carry

            lax.fori_loop(0, 16, block, 0)

        @pl.when(z == source_plane)
        def _():
            @pl.when(sends_halo)
            def _():
                halo(n).start()

            @pl.when(jnp.logical_not(sends_halo))
            def _():
                for x in range(8):
                    plane = state[n, 1 + z, x].astype(F32)
                    flux_out[n, x : x + 1, :] = speed_z * jnp.sum(plane, axis=0, keepdims=True)
                for k in range(8):
                    flux(n, k).start()

        for j in range(2):
            both = project(n, z, (1 - core) * 4 + 2 * j)
            sum_core_out[q, 2 * j] = both[:, :128].astype(BF16)
            sum_core_out[q, 2 * j + 1] = both[:, 128:].astype(BF16)
        message(CORE_SUM, q).start()
        for j in range(2):
            both = project(n, z, mine + 2 * j)
            part[q, 2 * j] = both[:, :128]
            part[q, 2 * j + 1] = both[:, 128:]

    def chip_sum(q, j):
        return part[q, j] + sum_core_in[q, j].astype(F32)

    def first_sums(q):
        message(CORE_SUM, q).wait_recv()
        sum_a_out[q, 0] = chip_sum(q, chip_o).astype(BF16)
        message(PASS_SUM, q).start()
        sum_a_out[q, 1] = chip_sum(q, chip_a).astype(BF16)
        message(NEAR_SUM, q).start()

    def second_sums(q):
        message(PASS_SUM, q).wait_recv()
        sum_b_out[q] = (chip_sum(q, chip_b) + sum_a_in[q, 0].astype(F32)).astype(BF16)
        message(LAST_SUM, q).start()

    def third_sums(q):
        message(NEAR_SUM, q).wait_recv()
        message(LAST_SUM, q).wait_recv()
        total = chip_sum(q, chip) + sum_a_in[q, 1].astype(F32) + sum_b_in[q].astype(F32)
        part[q, chip] = total
        sum_y_out[q] = total.astype(BF16)
        message(PAIR_SUM, q).start()

    def finish_sums(q):
        message(PAIR_SUM, q).wait_recv()
        coeffs[q, mine + chip] = (part[q, chip] + sum_y_in[q].astype(F32)).astype(BF16)
        message(OUT_B, q).start()
        message(OUT_A, q).start()

    def pass_on(q):
        message(OUT_B, q).wait_recv()
        message(OUT_PASS, q).start()

    def cross(q):
        message(OUT_A, q).wait_recv()
        message(OUT_PASS, q).wait_recv()
        message(CORE_OUT, q).start()

    def wall(n):
        for k in range(8):
            flux_arrival(n, k).wait_recv()
        line = (lax.broadcasted_iota(jnp.int32, (8, 128), 1).astype(F32) - MIDPOINT) * SPACING
        valid = lax.broadcasted_iota(jnp.int32, (8, 128), 1) < NV
        gauss = jnp.where(valid, jnp.exp(-0.5 * line * line), 0.0)
        flow = jnp.sum(jnp.maximum(line, 0.0) * gauss, axis=1, keepdims=True)
        mass = jnp.sum(gauss, axis=1, keepdims=True)
        norm = flow * mass * mass
        out = flux_in[n, 0]
        for k in range(1, 8):
            out = out + flux_in[n, k]
        kind = wall_ref[1 - upper]
        opened = jnp.where(kind == 2, 0.0, 1.0)
        sigma = out / norm * opened
        heating = jnp.where(kind == 1, wall_heat, 0.0)
        rows = lax.broadcasted_iota(jnp.int32, (256, 128), 0)
        one_x = ((rows >> 4).astype(F32) - MIDPOINT) * SPACING
        one_y = ((rows & 15).astype(F32) - MIDPOINT) * SPACING
        half_sq = 0.5 * (one_x * one_x + one_y * one_y + speed_z * speed_z)
        maxwell = jnp.exp(-half_sq)
        energy = half_sq - 1.5
        for x in range(8):
            ghost = maxwell * (sigma[x : x + 1] + heating[x : x + 1] * energy)
            state[n, halo_slot, x] = ghost.astype(BF16)

    def update(q):
        n, z = q // depth, level_of(q)
        message(CORE_OUT, q).wait_recv()

        @pl.when(z == target_plane)
        def _():
            @pl.when(takes_halo)
            def _():
                halo(n).wait_recv()

            @pl.when(jnp.logical_not(takes_halo))
            def _():
                wall(n)

        def row_pair(i, carry):
            pair = jnp.concatenate([coeffs[q, 2 * i], coeffs[q, 2 * i + 1]], axis=1)
            gained = jnp.dot(up_ref[...], pair, preferred_element_type=F32)
            for side in range(2):
                x = 2 * i + side
                for half in range(2):
                    rows = slice(128 * half, 128 * half + 128)
                    beside = lax.rem(x + (1 if half == 0 else 7), 8)
                    centre = state[n, 1 + z, x, rows].astype(F32)
                    wind_z = state[n, 1 + z - sign, x, rows].astype(F32)
                    wind_x = state[n, 1 + z, beside, rows].astype(F32)
                    split = centre.reshape(8, 16, 128)
                    wind_y = jnp.concatenate(
                        [pltpu.roll(split[:, :8], 127, 2), pltpu.roll(split[:, 8:], 1, 2)], axis=1
                    ).reshape(128, 128)
                    new = (
                        keep[rows] * centre
                        + slope_z * wind_z
                        + slope_x[rows] * wind_x
                        + slope_y[rows] * wind_y
                        + time_ratio * gained[rows, 128 * side : 128 * side + 128]
                    )
                    state[n + 1, 1 + z, x, rows] = new.astype(BF16)
            return carry

        lax.fori_loop(0, 4, row_pair, 0)

        @pl.when(q >= depth)
        def _():
            def block(i, carry):
                rows = pl.ds(pl.multiple_of(i * 16, 16), 16)
                raw[z, rows] = jnp.swapaxes(state[STEPS, 1 + z, :, rows, :], 0, 1)
                return carry

            lax.fori_loop(0, 16, block, 0)
            store(z).start()

    order = [
        (cross, 6),
        (pass_on, 5),
        (finish_sums, 4),
        (third_sums, 3),
        (second_sums, 2),
        (first_sums, 1),
        (update, 7),
        (begin, 0),
    ]

    def tick(t, carry):
        for act, lag in order:
            entry = t - lag
            q = entry - entry // (depth + 1)

            @pl.when((entry >= 0) & (entry <= chunks) & (entry != depth))
            def _(act=act, q=q):
                act(q)

        return carry

    lax.fori_loop(0, chunks + STAGES, tick, 0)

    def drain(q, carry):
        for kind in range(9):
            message(kind, q).wait_send()
        return carry

    lax.fori_loop(0, chunks, drain, 0)

    @pl.when(sends_halo)
    def _():
        for n in range(STEPS):
            halo(n).wait_send()

    @pl.when(jnp.logical_not(sends_halo))
    def _():
        for n in range(STEPS):
            for k in range(8):
                flux(n, k).wait_send()

    for z in range(depth):
        store(z).wait()


def body(slabs, distribution, up_factor, down_factor, decay, wall_kind):
    local_vel, depth, width_x, width_y = distribution.shape
    rank = up_factor.shape[1]
    chunks = STEPS * depth
    piece = (rank, width_y)
    vmem = pl.BlockSpec(memory_space=pltpu.VMEM)
    anywhere = pl.BlockSpec(memory_space=pl.ANY)
    dma = pltpu.SemaphoreType.DMA
    return pl.pallas_call(
        functools.partial(kernel, depth, slabs),
        out_shape=jax.ShapeDtypeStruct(distribution.shape, distribution.dtype),
        in_specs=[anywhere, vmem, vmem, vmem, vmem],
        out_specs=anywhere,
        scratch_shapes=[
            pltpu.VMEM((STEPS + 1, depth + 2, width_x, local_vel, width_y), BF16),
            pltpu.VMEM((depth, local_vel, width_x, width_y), BF16),
            pltpu.VMEM((rank, local_vel), BF16),
            pltpu.VMEM((local_vel, width_y), F32),
            pltpu.VMEM((local_vel, width_y), F32),
            pltpu.VMEM((local_vel, width_y), F32),
            pltpu.VMEM((chunks, 4) + piece, F32),
            pltpu.VMEM((chunks, 4) + piece, BF16),
            pltpu.VMEM((chunks, 4) + piece, BF16),
            pltpu.VMEM((chunks, 2) + piece, BF16),
            pltpu.VMEM((chunks, 2) + piece, BF16),
            pltpu.VMEM((chunks,) + piece, BF16),
            pltpu.VMEM((chunks,) + piece, BF16),
            pltpu.VMEM((chunks,) + piece, BF16),
            pltpu.VMEM((chunks,) + piece, BF16),
            pltpu.VMEM((chunks, 8) + piece, BF16),
            pltpu.VMEM((STEPS, width_x, width_y), F32),
            pltpu.VMEM((STEPS, 8, width_x, width_y), F32),
            dma((9, chunks)),
            dma((9, chunks)),
            dma((STEPS,)),
            dma((STEPS,)),
            dma((STEPS, 8)),
            dma((STEPS, 8)),
            dma((depth,)),
            dma((depth,)),
        ],
        compiler_params=pltpu.CompilerParams(
            collective_id=0, has_side_effects=True, vmem_limit_bytes=56 * 2**20
        ),
        cost_estimate=pl.CostEstimate(
            flops=4 * STEPS * local_vel * rank * depth * width_x * width_y,
            bytes_accessed=4 * distribution.size,
            transcendentals=0,
        ),
        name="boltzmann_steps",
    )(distribution, up_factor, down_factor, decay.reshape(2, -1), wall_kind)


def solution(mesh):
    return jax.shard_map(
        functools.partial(body, mesh.shape["space"]),
        mesh=mesh,
        in_specs=(P("vel", "space", None, None), P("vel", None), P("vel", None), P("vel"), P()),
        out_specs=P("vel", "space", None, None),
        check_vma=False,
    )
```

time: 420 us -> 103 us (0.25)
  waiting for transfers between devices: 181 us -> 0 us
  Pallas kernels: 0 us -> 98.7 us
  blocking collectives: 71.1 us -> 0 us
  other arithmetic: 69.8 us -> 0 us
  local copies, waits for them, and re-layouts: 53.4 us -> 4.09 us
  matrix products: 20.8 us -> 0 us
  between operations: 13.3 us -> 0.01 us
  starting transfers between devices: 8.72 us -> 0 us
    reduce_scatter x2 -> x0, waiting for transfers between devices: 181 us -> none  [body(): lax.psum_scatter(lax.dot_general(flat_rows, down_factor, (((0,), (0,)), (...]
    pallas_call x0 -> x1, Pallas kernels: none -> 98.7 us  [body(): pl.pallas_call(functools.partial(kernel, depth, slabs), out_shape=jax.Sha...]
    psum x2 -> x0, blocking collectives: 71.1 us -> none  [body(): outflux = lax.psum(jnp.stack([out_low, out_high]), 'vel')]
    convert_element_type x6 -> x0, other arithmetic: 57 us -> none  [the longest x2 44.2 us: body(): current = updated.astype(jnp.bfloat16)]
    slice x8 -> x0, local copies, waits for them, and re-layouts: 37.1 us -> none  [the longest x4 22 us: transport(): jnp.roll(centre, 1, axis_y)]
    dot_general x4 -> x0, matrix products: 20.8 us -> none  [the longest x2 11 us: body(): lax.dot_general(up_factor, lax.all_gather(coeffs, 'vel', axis=0, tiled=Tr...]
    reshape x2 -> x0, local copies, waits for them, and re-layouts: 13.4 us -> none  [body(): gained = lax.dot_general(up_factor, lax.all_gather(coeffs, 'vel', axis=0,...]
    select_n x3 -> x0, other arithmetic: 8.84 us -> none  [the longest x2 6.22 us: body(): jnp.where(slab == 0, ghost_low, padded[:, 0].astype(jnp.float32))]
  transfers between devices with their start and end apart: 8 -> 0, of which waited for: 2 -> 0; matrix products, arithmetic and copies ran while one was open for 15% -> 0% of each run, Pallas kernels for 0% -> 0%
where the time goes in v1:
time: 103 us
  Pallas kernels  98.7 us (96%)
  local copies, waits for them, and re-layouts  4.09 us (4%)
    pallas_call x1, Pallas kernels, body(): pl.pallas_call(functools.partial(kernel, depth, slabs), out_shape=jax.Sha...  98.7 us
    unnamed x1, local copies, waits for them, and re-layouts  4.09 us

profile of v1, /device:TPU:1, one launch (start us, length us, event | category | flops | bytes accessed | tf_op | source)
XLA Modules:
  0.0 102.8 jit_solution(6116165188289163210)
XLA Ops:
  0.0 98.7 %boltzmann_steps.1 = bf16[256,6,8,128]{3,2,1,0:T(8,128)(2,1)} custom-call(bf16[256,6,8,128]{3,2,1,0:T(8,128)(2,1)} %dist_ref.1, bf16[256,256]{1,0:T(8,128)(2,1)} %up_ref.1, bf16[256,256]{1,0:T(8,128)(2,1)} %down_ref.1, f32[2,128]{1,0:T(2,128)} %bitcast.1, s32[2,8,128]{2,1,0:T(8,128)} %wall_ref.1), custom_call_target="tpu_custom_call" | custom-call | flops 3221225472 | bytes 6291456 | tf_op jit(solution)/shard_map/boltzmann_steps/pallas_call | solution.py:407
  98.7 4.1 %copy.7 = bf16[256,6,8,128]{3,2,1,0:T(8,128)(2,1)} copy(bf16[256,6,8,128]{3,2,1,0:T(8,128)(2,1)} %boltzmann_steps.1) | data formatting | bytes 6291456

commit v2 on v1

v2 whole, which is shorter than its diff:
```python
import functools
from typing import Any, NamedTuple

import jax
import jax.numpy as jnp
from jax import lax
from jax.experimental import pallas as pl
from jax.experimental.pallas import tpu as pltpu
from jax.sharding import PartitionSpec as P

NV = 16
STEPS = 2
MESH = pl.DeviceIdType.MESH
VMEM_MIB = 56

speed_range = 8.0
time_ratio = 0.08
wall_heat = 3.0

SPACING = speed_range / NV
MIDPOINT = (NV - 1) / 2.0
F32 = jnp.float32
BF16 = jnp.bfloat16

CORE_SUM, PASS_SUM, NEAR_SUM, LAST_SUM, PAIR_SUM, OUT_B, OUT_A, OUT_PASS, CORE_OUT = range(9)
LAG_BEGIN, LAG_FIRST, LAG_SECOND, LAG_THIRD, LAG_FINISH, LAG_PASS, LAG_CROSS, LAG_UPDATE = (
    0, 1, 3, 5, 7, 9, 11, 12,
)
EDGE_TICK = 7


class Lane(NamedTuple):
    part: Any
    core_out: Any
    core_in: Any
    a_out: Any
    a_in: Any
    b_out: Any
    b_in: Any
    y_out: Any
    y_in: Any
    coeffs: Any
    send: Any
    recv: Any


def kernel(
    depth,
    slabs,
    dist_ref,
    up_ref,
    down_ref,
    decay_ref,
    wall_ref,
    out_ref,
    state,
    raw,
    down_t,
    mix,
    keep,
    slope_x,
    slope_y,
    flux_out,
    flux_in,
    halo_send,
    halo_recv,
    flux_send,
    flux_recv,
    in_sem,
    out_sem,
    *lane_refs,
):
    count = len(Lane._fields)
    cells = Lane(*lane_refs[:count])
    extra = Lane(*lane_refs[count:])
    chunks = STEPS * depth
    slab = lax.axis_index("space")
    vel = lax.axis_index("vel")
    core = lax.rem(vel, 2)
    chip = lax.rem(vel // 2, 4)
    upper = vel // 8
    sign = 2 * upper - 1
    flip = chip + 1 - 2 * lax.rem(chip, 2)
    mirror = 3 - chip
    chip_a = flip * (1 - core) + mirror * core
    chip_b = mirror * (1 - core) + flip * core
    chip_o = lax.rem(chip + 2, 4)

    def device(pair, x, c):
        return (slab, pair * 8 + x * 2 + c)

    to_core = device(upper, chip, 1 - core)
    to_a = device(upper, chip_a, core)
    to_b = device(upper, chip_b, core)
    to_pair = device(1 - upper, chip, core)
    to_slab = (lax.rem(slab + sign + slabs, slabs), vel)
    last = depth - 1
    source_plane = last * upper
    target_plane = last * (1 - upper)
    halo_slot = (depth + 1) * (1 - upper)
    sends_halo = slab != (slabs - 1) * upper
    takes_halo = slab != (slabs - 1) * (1 - upper)
    mine = core * 4
    theirs = 4 - mine

    def level_of(q):
        return lax.rem(2 * depth - q + (depth - 2) * (q // depth), depth)

    def load(z):
        return pltpu.make_async_copy(dist_ref.at[:, z], raw.at[z], in_sem.at[z])

    def store(z):
        return pltpu.make_async_copy(raw.at[z], out_ref.at[:, z], out_sem.at[z])

    def message(kind, lane, q):
        own = lane.coeffs.at[q, mine + chip]
        if kind == CORE_SUM:
            src, dst, target = lane.core_out.at[q], lane.core_in.at[q], to_core
        elif kind == PASS_SUM:
            src, dst, target = lane.a_out.at[q, 0], lane.a_in.at[q, 0], to_a
        elif kind == NEAR_SUM:
            src, dst, target = lane.a_out.at[q, 1], lane.a_in.at[q, 1], to_a
        elif kind == LAST_SUM:
            src, dst, target = lane.b_out.at[q], lane.b_in.at[q], to_b
        elif kind == PAIR_SUM:
            src, dst, target = lane.y_out.at[q], lane.y_in.at[q], to_pair
        elif kind == OUT_B:
            src, dst, target = own, own, to_b
        elif kind == OUT_A:
            src, dst, target = own, own, to_a
        elif kind == OUT_PASS:
            src = lane.coeffs.at[q, mine + chip_b]
            dst, target = src, to_a
        else:
            src = lane.coeffs.at[q, pl.ds(mine, 4)]
            dst, target = src, to_core
        return pltpu.make_async_remote_copy(
            src_ref=src,
            dst_ref=dst,
            send_sem=lane.send.at[kind, q],
            recv_sem=lane.recv.at[kind, q],
            device_id=target,
            device_id_type=MESH,
        )

    def halo(n):
        return pltpu.make_async_remote_copy(
            src_ref=state.at[n, 1 + source_plane],
            dst_ref=state.at[n, halo_slot],
            send_sem=halo_send.at[n],
            recv_sem=halo_recv.at[n],
            device_id=to_slab,
            device_id_type=MESH,
        )

    def flux(n, k, sender):
        return pltpu.make_async_remote_copy(
            src_ref=flux_out.at[n],
            dst_ref=flux_in.at[n, sender],
            send_sem=flux_send.at[n, k],
            recv_sem=flux_recv.at[n, sender],
            device_id=(slab, (1 - upper) * 8 + k),
            device_id_type=MESH,
        )

    for q in range(depth):
        load((depth - q) % depth).start()

    barrier = pltpu.get_barrier_semaphore()

    def greet(target):
        pl.semaphore_signal(barrier, inc=1, device_id=target, device_id_type=MESH)

    for target in (to_core, to_a, to_b):
        greet(target)
    for k in range(8):
        greet((slab, (1 - upper) * 8 + k))
    greet((lax.rem(slab + slabs - 1, slabs), vel))
    greet((lax.rem(slab + 1, slabs), vel))

    down_t[...] = down_ref[...].T
    for j in range(4):
        for base, left in ((theirs, True), (mine, False)):
            rows = pl.ds(pl.multiple_of((base + j) * 32, 32), 32)
            both = jnp.dot(down_t[rows, :], up_ref[...], preferred_element_type=F32)
            for side in range(2):
                value = both[:, 128 * side : 128 * side + 128]
                if left:
                    extra.core_out[0, j, 32 * side : 32 * side + 32] = value.astype(BF16)
                else:
                    extra.part[0, j, 32 * side : 32 * side + 32] = value
    ids = lax.broadcasted_iota(jnp.int32, (256, 128), 0)
    speed_x = jnp.abs(((ids >> 4).astype(F32) - MIDPOINT) * SPACING)
    speed_y = jnp.abs(((ids & 15).astype(F32) - MIDPOINT) * SPACING)
    speed_z = jnp.abs((vel.astype(F32) - MIDPOINT) * SPACING)
    decay = jnp.concatenate(
        [jnp.broadcast_to(decay_ref[i : i + 1, :], (128, 128)).T for i in range(2)], axis=0
    )
    keep[...] = 1.0 - time_ratio * (speed_x + speed_y + speed_z + decay)
    slope_x[...] = time_ratio * speed_x
    slope_y[...] = time_ratio * speed_y
    slope_z = time_ratio * speed_z

    def arrange(q, carry):
        z = level_of(q)
        load(z).wait()

        def block(i, inner):
            rows = pl.ds(pl.multiple_of(i * 16, 16), 16)
            state[0, 1 + z, :, rows, :] = jnp.swapaxes(raw[z, rows], 0, 1)
            return inner

        return lax.fori_loop(0, 16, block, carry)

    lax.fori_loop(0, depth, arrange, 0)
    pl.semaphore_wait(barrier, 13)

    def send_edge(n):
        @pl.when(sends_halo)
        def _():
            halo(n).start()

        @pl.when(jnp.logical_not(sends_halo))
        def _():
            for x in range(8):
                plane = state[n, 1 + source_plane, x].astype(F32)
                flux_out[n, x : x + 1, :] = speed_z * jnp.sum(plane, axis=0, keepdims=True)
            for k in range(8):
                flux(n, k, chip * 2 + core).start()

    def take_edge(n):
        @pl.when(takes_halo)
        def _():
            halo(n).wait_recv()

        @pl.when(jnp.logical_not(takes_halo))
        def _():
            wall(n)

    def wall(n):
        for k in range(8):
            flux(n, k, k).wait_recv()
        line = (lax.broadcasted_iota(jnp.int32, (8, 128), 1).astype(F32) - MIDPOINT) * SPACING
        valid = lax.broadcasted_iota(jnp.int32, (8, 128), 1) < NV
        gauss = jnp.where(valid, jnp.exp(-0.5 * line * line), 0.0)
        flow = jnp.sum(jnp.maximum(line, 0.0) * gauss, axis=1, keepdims=True)
        mass = jnp.sum(gauss, axis=1, keepdims=True)
        norm = flow * mass * mass
        out = flux_in[n, 0]
        for k in range(1, 8):
            out = out + flux_in[n, k]
        kind = wall_ref[1 - upper]
        opened = jnp.where(kind == 2, 0.0, 1.0)
        sigma = out / norm * opened
        heating = jnp.where(kind == 1, wall_heat, 0.0)
        rows = lax.broadcasted_iota(jnp.int32, (256, 128), 0)
        one_x = ((rows >> 4).astype(F32) - MIDPOINT) * SPACING
        one_y = ((rows & 15).astype(F32) - MIDPOINT) * SPACING
        half_sq = 0.5 * (one_x * one_x + one_y * one_y + speed_z * speed_z)
        maxwell = jnp.exp(-half_sq)
        energy = half_sq - 1.5
        for x in range(8):
            ghost = maxwell * (sigma[x : x + 1] + heating[x : x + 1] * energy)
            state[n, halo_slot, x] = ghost.astype(BF16)

    def drift(n, z, x, half):
        rows = slice(128 * half, 128 * half + 128)
        beside = lax.rem(x + (1 if half == 0 else 7), 8)
        centre = state[n, 1 + z, x, rows].astype(F32)
        wind_z = state[n, 1 + z - sign, x, rows].astype(F32)
        wind_x = state[n, 1 + z, beside, rows].astype(F32)
        split = centre.reshape(8, 16, 128)
        wind_y = jnp.concatenate(
            [pltpu.roll(split[:, :8], 127, 2), pltpu.roll(split[:, 8:], 1, 2)], axis=1
        ).reshape(128, 128)
        return (
            keep[rows] * centre
            + slope_z * wind_z
            + slope_x[rows] * wind_x
            + slope_y[rows] * wind_y
        )

    def begin(q):
        n, z = q // depth, level_of(q)

        @pl.when(q >= depth)
        def _():
            def row(x, carry):
                for half in range(2):
                    rows = slice(128 * half, 128 * half + 128)
                    state[STEPS, 1 + z, x, rows] = drift(0, z, x, half).astype(BF16)
                return carry

            lax.fori_loop(0, 8, row, 0)

        def project(x):
            pair = jnp.concatenate(
                [state[STEPS * n, 1 + z, x], state[STEPS * n, 1 + z, x + 1]], axis=1
            )
            return jnp.dot(down_t[...], pair, preferred_element_type=F32)

        for j in range(2):
            both = project(theirs + 2 * j)
            cells.core_out[q, 2 * j] = both[:, :128].astype(BF16)
            cells.core_out[q, 2 * j + 1] = both[:, 128:].astype(BF16)
        message(CORE_SUM, cells, q).start()
        for j in range(2):
            both = project(mine + 2 * j)
            cells.part[q, 2 * j] = both[:, :128]
            cells.part[q, 2 * j + 1] = both[:, 128:]

    def chip_sum(lane, q, j):
        return lane.part[q, j] + lane.core_in[q, j].astype(F32)

    def first_sums(lane, q):
        message(CORE_SUM, lane, q).wait_recv()
        lane.a_out[q, 0] = chip_sum(lane, q, chip_o).astype(BF16)
        message(PASS_SUM, lane, q).start()
        lane.a_out[q, 1] = chip_sum(lane, q, chip_a).astype(BF16)
        message(NEAR_SUM, lane, q).start()

    def second_sums(lane, q):
        message(PASS_SUM, lane, q).wait_recv()
        total = chip_sum(lane, q, chip_b) + lane.a_in[q, 0].astype(F32)
        lane.b_out[q] = total.astype(BF16)
        message(LAST_SUM, lane, q).start()

    def third_sums(lane, q):
        message(NEAR_SUM, lane, q).wait_recv()
        message(LAST_SUM, lane, q).wait_recv()
        total = chip_sum(lane, q, chip) + lane.a_in[q, 1].astype(F32)
        total = total + lane.b_in[q].astype(F32)
        lane.part[q, chip] = total
        lane.y_out[q] = total.astype(BF16)
        message(PAIR_SUM, lane, q).start()

    def finish_sums(lane, q):
        message(PAIR_SUM, lane, q).wait_recv()
        if lane is cells:

            @pl.when(q >= depth)
            def _():
                before = lax.rem(depth - level_of(q), depth)
                known = lane.coeffs[before, mine + chip]
                gain = jnp.dot(mix[...], known, preferred_element_type=F32)
                lane.part[q, chip] += time_ratio * gain

        total = lane.part[q, chip] + lane.y_in[q].astype(F32)
        lane.coeffs[q, mine + chip] = total.astype(BF16)
        message(OUT_B, lane, q).start()
        message(OUT_A, lane, q).start()

    def pass_on(lane, q):
        message(OUT_B, lane, q).wait_recv()
        message(OUT_PASS, lane, q).start()

    def cross(lane, q):
        message(OUT_A, lane, q).wait_recv()
        message(OUT_PASS, lane, q).wait_recv()
        message(CORE_OUT, lane, q).start()

    def finish_mix():
        message(CORE_OUT, extra, 0).wait_recv()
        for j in range(8):
            for side in range(2):
                piece = extra.coeffs[0, j, 32 * side : 32 * side + 32]
                mix[32 * j : 32 * j + 32, 128 * side : 128 * side + 128] = piece

    def update(q):
        n, z = q // depth, level_of(q)
        message(CORE_OUT, cells, q).wait_recv()

        @pl.when((q >= depth) & (z == target_plane))
        def _():
            take_edge(1)

        def row_pair(i, carry):
            pair = jnp.concatenate([cells.coeffs[q, 2 * i], cells.coeffs[q, 2 * i + 1]], axis=1)
            gained = jnp.dot(up_ref[...], pair, preferred_element_type=F32)
            for side in range(2):
                x = 2 * i + side
                for half in range(2):
                    rows = slice(128 * half, 128 * half + 128)
                    new = (
                        drift(n, z, x, half)
                        + time_ratio * gained[rows, 128 * side : 128 * side + 128]
                    )
                    state[n + 1, 1 + z, x, rows] = new.astype(BF16)
            return carry

        lax.fori_loop(0, 4, row_pair, 0)

        @pl.when((q < depth) & (z == source_plane))
        def _():
            send_edge(1)

        @pl.when(q >= depth)
        def _():
            def block(i, carry):
                rows = pl.ds(pl.multiple_of(i * 16, 16), 16)
                raw[z, rows] = jnp.swapaxes(state[STEPS, 1 + z, :, rows, :], 0, 1)
                return carry

            lax.fori_loop(0, 16, block, 0)
            store(z).start()

    order = [
        (cross, LAG_CROSS),
        (pass_on, LAG_PASS),
        (finish_sums, LAG_FINISH),
        (third_sums, LAG_THIRD),
        (second_sums, LAG_SECOND),
        (first_sums, LAG_FIRST),
    ]

    def tick(t, carry):
        @pl.when(t == LAG_UPDATE)
        def _():
            finish_mix()

        for act, lag in order:

            @pl.when(t == lag)
            def _(act=act):
                act(extra, 0)

            @pl.when((t >= lag) & (t < lag + chunks))
            def _(act=act, lag=lag):
                act(cells, t - lag)

        @pl.when(t == EDGE_TICK)
        def _():
            take_edge(0)

        @pl.when(t >= LAG_UPDATE)
        def _():
            update(t - LAG_UPDATE)

        @pl.when(t < chunks)
        def _():
            begin(t)

        return carry

    message(CORE_SUM, extra, 0).start()
    send_edge(0)
    lax.fori_loop(0, chunks + LAG_UPDATE, tick, 0)

    def drain(q, carry):
        for kind in range(9):
            message(kind, cells, q).wait_send()
        return carry

    lax.fori_loop(0, chunks, drain, 0)
    for kind in range(9):
        message(kind, extra, 0).wait_send()

    @pl.when(sends_halo)
    def _():
        for n in range(STEPS):
            halo(n).wait_send()

    @pl.when(jnp.logical_not(sends_halo))
    def _():
        for n in range(STEPS):
            for k in range(8):
                flux(n, k, chip * 2 + core).wait_send()

    for z in range(depth):
        store(z).wait()


def lane_shapes(chunks, piece):
    def vmem(lead, kind):
        return pltpu.VMEM((chunks,) + lead + piece, kind)

    return Lane(
        part=vmem((4,), F32),
        core_out=vmem((4,), BF16),
        core_in=vmem((4,), BF16),
        a_out=vmem((2,), BF16),
        a_in=vmem((2,), BF16),
        b_out=vmem((), BF16),
        b_in=vmem((), BF16),
        y_out=vmem((), BF16),
        y_in=vmem((), BF16),
        coeffs=vmem((8,), BF16),
        send=pltpu.SemaphoreType.DMA((9, chunks)),
        recv=pltpu.SemaphoreType.DMA((9, chunks)),
    )


def body(slabs, distribution, up_factor, down_factor, decay, wall_kind):
    local_vel, depth, width_x, width_y = distribution.shape
    rank = up_factor.shape[1]
    vmem = pl.BlockSpec(memory_space=pltpu.VMEM)
    anywhere = pl.BlockSpec(memory_space=pl.ANY)
    dma = pltpu.SemaphoreType.DMA
    return pl.pallas_call(
        functools.partial(kernel, depth, slabs),
        out_shape=jax.ShapeDtypeStruct(distribution.shape, distribution.dtype),
        in_specs=[anywhere, vmem, vmem, vmem, vmem],
        out_specs=anywhere,
        scratch_shapes=[
            pltpu.VMEM((STEPS + 1, depth + 2, width_x, local_vel, width_y), BF16),
            pltpu.VMEM((depth, local_vel, width_x, width_y), BF16),
            pltpu.VMEM((rank, local_vel), BF16),
            pltpu.VMEM((rank, rank), BF16),
            pltpu.VMEM((local_vel, width_y), F32),
            pltpu.VMEM((local_vel, width_y), F32),
            pltpu.VMEM((local_vel, width_y), F32),
            pltpu.VMEM((STEPS, width_x, width_y), F32),
            pltpu.VMEM((STEPS, 8, width_x, width_y), F32),
            dma((STEPS,)),
            dma((STEPS,)),
            dma((STEPS, 8)),
            dma((STEPS, 8)),
            dma((depth,)),
            dma((depth,)),
            *lane_shapes(STEPS * depth, (rank, width_y)),
            *lane_shapes(1, (rank // 4, width_y)),
        ],
        compiler_params=pltpu.CompilerParams(
            collective_id=0, has_side_effects=True, vmem_limit_bytes=VMEM_MIB * 2**20
        ),
        cost_estimate=pl.CostEstimate(
            flops=4 * STEPS * local_vel * rank * depth * width_x * width_y,
            bytes_accessed=4 * distribution.size,
            transcendentals=0,
        ),
        name="boltzmann_steps",
    )(distribution, up_factor, down_factor, decay.reshape(2, -1), wall_kind)


def solution(mesh):
    return jax.shard_map(
        functools.partial(body, mesh.shape["space"]),
        mesh=mesh,
        in_specs=(P("vel", "space", None, None), P("vel", None), P("vel", None), P("vel"), P()),
        out_specs=P("vel", "space", None, None),
        check_vma=False,
    )
```

time: 103 us -> 84.9 us (0.82)
  Pallas kernels: 98.7 us -> 80.7 us
    pallas_call x1, Pallas kernels: 98.7 us -> 80.7 us  [body(): pl.pallas_call(functools.partial(kernel, depth, slabs), out_shape=jax.Sha...]
where the time goes in v2:
time: 84.9 us; the launch traced here: 84.8 us
  Pallas kernels  80.7 us (95%)
  local copies, waits for them, and re-layouts  4.09 us (5%)
    pallas_call x1, Pallas kernels, body(): pl.pallas_call(functools.partial(kernel, depth, slabs), out_shape=jax.Sha...  80.7 us
    unnamed x1, local copies, waits for them, and re-layouts  4.09 us

profile of v2, /device:TPU:1, one launch (start us, length us, event | category | flops | bytes accessed | tf_op | source)
XLA Modules:
  0.0 84.8 jit_solution(6707186227954021217)
XLA Ops:
  0.0 80.7 %boltzmann_steps.1 = bf16[256,6,8,128]{3,2,1,0:T(8,128)(2,1)} custom-call(bf16[256,6,8,128]{3,2,1,0:T(8,128)(2,1)} %dist_ref.1, bf16[256,256]{1,0:T(8,128)(2,1)} %up_ref.1, bf16[256,256]{1,0:T(8,128)(2,1)} %down_ref.1, f32[2,128]{1,0:T(2,128)} %bitcast.1, s32[2,8,128]{2,1,0:T(8,128)} %wall_ref.1), custom_call_target="tpu_custom_call" | custom-call | flops 3221225472 | bytes 6291456 | tf_op jit(solution)/shard_map/boltzmann_steps/pallas_call | solution.py:499
  80.7 4.1 %copy.7 = bf16[256,6,8,128]{3,2,1,0:T(8,128)(2,1)} copy(bf16[256,6,8,128]{3,2,1,0:T(8,128)(2,1)} %boltzmann_steps.1) | data formatting | bytes 6291456

commit v3 on v2

--- a/solution.py
+++ b/solution.py
@@ -26,7 +26,7 @@
 LAG_BEGIN, LAG_FIRST, LAG_SECOND, LAG_THIRD, LAG_FINISH, LAG_PASS, LAG_CROSS, LAG_UPDATE = (
     0, 1, 3, 5, 7, 9, 11, 12,
 )
-EDGE_TICK = 7
+EDGE_TICK = 10
 
 
 class Lane(NamedTuple):
@@ -67,7 +67,6 @@
     flux_send,
     flux_recv,
     in_sem,
-    out_sem,
     *lane_refs,
 ):
     count = len(Lane._fields)
@@ -108,9 +107,6 @@
 
     def load(z):
         return pltpu.make_async_copy(dist_ref.at[:, z], raw.at[z], in_sem.at[z])
-
-    def store(z):
-        return pltpu.make_async_copy(raw.at[z], out_ref.at[:, z], out_sem.at[z])
 
     def message(kind, lane, q):
         own = lane.coeffs.at[q, mine + chip]
@@ -143,12 +139,12 @@
             device_id_type=MESH,
         )
 
-    def halo(n):
+    def halo(n, x):
         return pltpu.make_async_remote_copy(
-            src_ref=state.at[n, 1 + source_plane],
-            dst_ref=state.at[n, halo_slot],
-            send_sem=halo_send.at[n],
-            recv_sem=halo_recv.at[n],
+            src_ref=state.at[n, 1 + source_plane, x],
+            dst_ref=state.at[n, halo_slot, x],
+            send_sem=halo_send.at[n, x],
+            recv_sem=halo_recv.at[n, x],
             device_id=to_slab,
             device_id_type=MESH,
         )
@@ -215,11 +211,12 @@
     lax.fori_loop(0, depth, arrange, 0)
     pl.semaphore_wait(barrier, 13)
 
-    def send_edge(n):
+    def send_row(n, x):
         @pl.when(sends_halo)
         def _():
-            halo(n).start()
-
+            halo(n, x).start()
+
+    def send_flux(n):
         @pl.when(jnp.logical_not(sends_halo))
         def _():
             for x in range(8):
@@ -231,7 +228,8 @@
     def take_edge(n):
         @pl.when(takes_halo)
         def _():
-            halo(n).wait_recv()
+            for x in range(8):
+                halo(n, x).wait_recv()
 
         @pl.when(jnp.logical_not(takes_halo))
         def _():
@@ -392,17 +390,16 @@
 
         @pl.when((q < depth) & (z == source_plane))
         def _():
-            send_edge(1)
+            send_flux(1)
 
         @pl.when(q >= depth)
         def _():
             def block(i, carry):
                 rows = pl.ds(pl.multiple_of(i * 16, 16), 16)
-                raw[z, rows] = jnp.swapaxes(state[STEPS, 1 + z, :, rows, :], 0, 1)
+                out_ref[rows, z] = jnp.swapaxes(state[STEPS, 1 + z, :, rows, :], 0, 1)
                 return carry
 
             lax.fori_loop(0, 16, block, 0)
-            store(z).start()
 
     order = [
         (cross, LAG_CROSS),
@@ -428,6 +425,15 @@
             def _(act=act, lag=lag):
                 act(cells, t - lag)
 
+        @pl.when(t < 8)
+        def _():
+            send_row(0, t)
+
+        @pl.when((t >= LAG_UPDATE + 2) & (t < LAG_UPDATE + 6))
+        def _():
+            for side in range(2):
+                send_row(1, 2 * (t - LAG_UPDATE - 2) + side)
+
         @pl.when(t == EDGE_TICK)
         def _():
             take_edge(0)
@@ -443,7 +449,7 @@
         return carry
 
     message(CORE_SUM, extra, 0).start()
-    send_edge(0)
+    send_flux(0)
     lax.fori_loop(0, chunks + LAG_UPDATE, tick, 0)
 
     def drain(q, carry):
@@ -458,16 +464,14 @@
     @pl.when(sends_halo)
     def _():
         for n in range(STEPS):
-            halo(n).wait_send()
+            for x in range(8):
+                halo(n, x).wait_send()
 
     @pl.when(jnp.logical_not(sends_halo))
     def _():
         for n in range(STEPS):
             for k in range(8):
                 flux(n, k, chip * 2 + core).wait_send()
-
-    for z in range(depth):
-        store(z).wait()
 
 
 def lane_shapes(chunks, piece):
@@ -498,9 +502,9 @@
     dma = pltpu.SemaphoreType.DMA
     return pl.pallas_call(
         functools.partial(kernel, depth, slabs),
-        out_shape=jax.ShapeDtypeStruct(distribution.shape, distribution.dtype),
+        out_shape=pltpu.VMEM(distribution.shape, distribution.dtype),
         in_specs=[anywhere, vmem, vmem, vmem, vmem],
-        out_specs=anywhere,
+        out_specs=vmem,
         scratch_shapes=[
             pltpu.VMEM((STEPS + 1, depth + 2, width_x, local_vel, width_y), BF16),
             pltpu.VMEM((depth, local_vel, width_x, width_y), BF16),
@@ -511,11 +515,10 @@
             pltpu.VMEM((local_vel, width_y), F32),
             pltpu.VMEM((STEPS, width_x, width_y), F32),
             pltpu.VMEM((STEPS, 8, width_x, width_y), F32),
-            dma((STEPS,)),
-            dma((STEPS,)),
             dma((STEPS, 8)),
             dma((STEPS, 8)),
-            dma((depth,)),
+            dma((STEPS, 8)),
+            dma((STEPS, 8)),
             dma((depth,)),
             *lane_shapes(STEPS * depth, (rank, width_y)),
             *lane_shapes(1, (rank // 4, width_y)),

time: 84.9 us -> 77.5 us (0.913)
  Pallas kernels: 80.7 us -> 75.7 us
  local copies, waits for them, and re-layouts: 4.09 us -> 1.67 us
    pallas_call x1, Pallas kernels: 80.7 us -> 75.7 us  [body(): pl.pallas_call(functools.partial(kernel, depth, slabs), out_shape=pltpu.V...]
    unnamed x1, local copies, waits for them, and re-layouts: 4.09 us -> 1.67 us
where the time goes in v3:
time: 77.5 us; the launch traced here: 77.3 us
  Pallas kernels  75.7 us (98%)
  local copies, waits for them, and re-layouts  1.67 us (2%)
    pallas_call x1, Pallas kernels, body(): pl.pallas_call(functools.partial(kernel, depth, slabs), out_shape=pltpu.V...  75.7 us
    unnamed x1, local copies, waits for them, and re-layouts  1.67 us

profile of v3, /device:TPU:1, one launch (start us, length us, event | category | flops | bytes accessed | tf_op | source)
XLA Modules:
  0.0 77.3 jit_solution(15994711075023611592)
XLA Ops:
  0.0 75.7 %boltzmann_steps.1 = bf16[256,6,8,128]{3,2,1,0:T(8,128)(2,1)S(1)} custom-call(bf16[256,6,8,128]{3,2,1,0:T(8,128)(2,1)} %dist_ref.1, bf16[256,256]{1,0:T(8,128)(2,1)} %up_ref.1, bf16[256,256]{1,0:T(8,128)(2,1)} %down_ref.1, f32[2,128]{1,0:T(2,128)} %bitcast.1, s32[2,8,128]{2,1,0:T(8,128)} %wall_ref.1), custom_call_target="tpu_custom_call" | custom-call | flops 3221225472 | bytes 6291456 | tf_op jit(solution)/shard_map/boltzmann_steps/pallas_call | solution.py:503
  75.7 1.7 %copy.7 = bf16[256,6,8,128]{3,2,1,0:T(8,128)(2,1)} copy(bf16[256,6,8,128]{3,2,1,0:T(8,128)(2,1)S(1)} %boltzmann_steps.1) | data formatting | bytes 6291456

commit v4 on v3

--- a/solution.py
+++ b/solution.py
@@ -23,10 +23,10 @@
 BF16 = jnp.bfloat16
 
 CORE_SUM, PASS_SUM, NEAR_SUM, LAST_SUM, PAIR_SUM, OUT_B, OUT_A, OUT_PASS, CORE_OUT = range(9)
-LAG_BEGIN, LAG_FIRST, LAG_SECOND, LAG_THIRD, LAG_FINISH, LAG_PASS, LAG_CROSS, LAG_UPDATE = (
-    0, 1, 3, 5, 7, 9, 11, 12,
+LAG_FIRST, LAG_SECOND, LAG_THIRD, LAG_FINISH, LAG_PASS, LAG_CROSS, LAG_UPDATE = (
+    1, 3, 6, 9, 12, 14, 15,
 )
-EDGE_TICK = 10
+EDGE_TICK = 9
 
 
 class Lane(NamedTuple):
@@ -167,12 +167,17 @@
     def greet(target):
         pl.semaphore_signal(barrier, inc=1, device_id=target, device_id_type=MESH)
 
-    for target in (to_core, to_a, to_b):
+    for target in (to_core, to_a, to_b, to_pair):
         greet(target)
-    for k in range(8):
-        greet((slab, (1 - upper) * 8 + k))
-    greet((lax.rem(slab + slabs - 1, slabs), vel))
-    greet((lax.rem(slab + 1, slabs), vel))
+
+    @pl.when(takes_halo)
+    def _():
+        greet((slab - sign, vel))
+
+    @pl.when(jnp.logical_not(takes_halo))
+    def _():
+        for k in range(1, 8):
+            greet((slab, (1 - upper) * 8 + lax.rem(chip * 2 + core + k, 8)))
 
     down_t[...] = down_ref[...].T
     for j in range(4):
@@ -209,7 +214,6 @@
         return lax.fori_loop(0, 16, block, carry)
 
     lax.fori_loop(0, depth, arrange, 0)
-    pl.semaphore_wait(barrier, 13)
 
     def send_row(n, x):
         @pl.when(sends_halo)
@@ -301,7 +305,6 @@
             both = project(theirs + 2 * j)
             cells.core_out[q, 2 * j] = both[:, :128].astype(BF16)
             cells.core_out[q, 2 * j + 1] = both[:, 128:].astype(BF16)
-        message(CORE_SUM, cells, q).start()
         for j in range(2):
             both = project(mine + 2 * j)
             cells.part[q, 2 * j] = both[:, :128]
@@ -411,6 +414,10 @@
     ]
 
     def tick(t, carry):
+        @pl.when(t < chunks)
+        def _():
+            message(CORE_SUM, cells, t).start()
+
         @pl.when(t == LAG_UPDATE)
         def _():
             finish_mix()
@@ -442,12 +449,14 @@
         def _():
             update(t - LAG_UPDATE)
 
-        @pl.when(t < chunks)
-        def _():
-            begin(t)
+        @pl.when(t < chunks - 1)
+        def _():
+            begin(t + 1)
 
         return carry
 
+    begin(0)
+    pl.semaphore_wait(barrier, jnp.where(sends_halo, 5, 11))
     message(CORE_SUM, extra, 0).start()
     send_flux(0)
     lax.fori_loop(0, chunks + LAG_UPDATE, tick, 0)

time: 77.5 us -> 72.8 us (0.939)
  Pallas kernels: 75.7 us -> 71 us
    pallas_call x1, Pallas kernels: 75.7 us -> 71 us  [body(): pl.pallas_call(functools.partial(kernel, depth, slabs), out_shape=pltpu.V...]
where the time goes in v4:
time: 72.8 us; the launch traced here: 72.7 us
  Pallas kernels  71 us (98%)
  local copies, waits for them, and re-layouts  1.67 us (2%)
    pallas_call x1, Pallas kernels, body(): pl.pallas_call(functools.partial(kernel, depth, slabs), out_shape=pltpu.V...  71 us
    unnamed x1, local copies, waits for them, and re-layouts  1.67 us

profile of v4, /device:TPU:1, one launch (start us, length us, event | category | flops | bytes accessed | tf_op | source)
XLA Modules:
  0.0 72.7 jit_solution(17817526486878884259)
XLA Ops:
  0.0 71.0 %boltzmann_steps.1 = bf16[256,6,8,128]{3,2,1,0:T(8,128)(2,1)S(1)} custom-call(bf16[256,6,8,128]{3,2,1,0:T(8,128)(2,1)} %dist_ref.1, bf16[256,256]{1,0:T(8,128)(2,1)} %up_ref.1, bf16[256,256]{1,0:T(8,128)(2,1)} %down_ref.1, f32[2,128]{1,0:T(2,128)} %bitcast.1, s32[2,8,128]{2,1,0:T(8,128)} %wall_ref.1), custom_call_target="tpu_custom_call" | custom-call | flops 3221225472 | bytes 6291456 | tf_op jit(solution)/shard_map/boltzmann_steps/pallas_call | solution.py:512
  71.0 1.7 %copy.7 = bf16[256,6,8,128]{3,2,1,0:T(8,128)(2,1)} copy(bf16[256,6,8,128]{3,2,1,0:T(8,128)(2,1)S(1)} %boltzmann_steps.1) | data formatting | bytes 6291456

commit v5 on v4

--- a/solution.py
+++ b/solution.py
@@ -24,9 +24,10 @@
 
 CORE_SUM, PASS_SUM, NEAR_SUM, LAST_SUM, PAIR_SUM, OUT_B, OUT_A, OUT_PASS, CORE_OUT = range(9)
 LAG_FIRST, LAG_SECOND, LAG_THIRD, LAG_FINISH, LAG_PASS, LAG_CROSS, LAG_UPDATE = (
-    1, 3, 6, 9, 12, 14, 15,
+    0, 2, 5, 8, 11, 13, 14,
 )
-EDGE_TICK = 9
+EDGE_TICK = 8
+AHEAD = 2
 
 
 class Lane(NamedTuple):
@@ -159,9 +160,6 @@
             device_id_type=MESH,
         )
 
-    for q in range(depth):
-        load((depth - q) % depth).start()
-
     barrier = pltpu.get_barrier_semaphore()
 
     def greet(target):
@@ -178,6 +176,9 @@
     def _():
         for k in range(1, 8):
             greet((slab, (1 - upper) * 8 + lax.rem(chip * 2 + core + k, 8)))
+
+    for q in range(depth):
+        load((depth - q) % depth).start()
 
     down_t[...] = down_ref[...].T
     for j in range(4):
@@ -367,19 +368,15 @@
                 piece = extra.coeffs[0, j, 32 * side : 32 * side + 32]
                 mix[32 * j : 32 * j + 32, 128 * side : 128 * side + 128] = piece
 
-    def update(q):
+    def update_rows(q, base):
         n, z = q // depth, level_of(q)
-        message(CORE_OUT, cells, q).wait_recv()
-
-        @pl.when((q >= depth) & (z == target_plane))
-        def _():
-            take_edge(1)
 
         def row_pair(i, carry):
-            pair = jnp.concatenate([cells.coeffs[q, 2 * i], cells.coeffs[q, 2 * i + 1]], axis=1)
+            first = base + 2 * i
+            pair = jnp.concatenate([cells.coeffs[q, first], cells.coeffs[q, first + 1]], axis=1)
             gained = jnp.dot(up_ref[...], pair, preferred_element_type=F32)
             for side in range(2):
-                x = 2 * i + side
+                x = first + side
                 for half in range(2):
                     rows = slice(128 * half, 128 * half + 128)
                     new = (
@@ -389,7 +386,19 @@
                     state[n + 1, 1 + z, x, rows] = new.astype(BF16)
             return carry
 
-        lax.fori_loop(0, 4, row_pair, 0)
+        lax.fori_loop(0, 2, row_pair, 0)
+
+    def update_own(q):
+        @pl.when((q >= depth) & (level_of(q) == target_plane))
+        def _():
+            take_edge(1)
+
+        update_rows(q, mine)
+
+    def update_rest(q):
+        z = level_of(q)
+        message(CORE_OUT, cells, q).wait_recv()
+        update_rows(q, theirs)
 
         @pl.when((q < depth) & (z == source_plane))
         def _():
@@ -414,10 +423,6 @@
     ]
 
     def tick(t, carry):
-        @pl.when(t < chunks)
-        def _():
-            message(CORE_SUM, cells, t).start()
-
         @pl.when(t == LAG_UPDATE)
         def _():
             finish_mix()
@@ -432,9 +437,10 @@
             def _(act=act, lag=lag):
                 act(cells, t - lag)
 
-        @pl.when(t < 8)
-        def _():
-            send_row(0, t)
+        @pl.when(t < 4)
+        def _():
+            for side in range(2):
+                send_row(0, 2 * t + side)
 
         @pl.when((t >= LAG_UPDATE + 2) & (t < LAG_UPDATE + 6))
         def _():
@@ -447,17 +453,28 @@
 
         @pl.when(t >= LAG_UPDATE)
         def _():
-            update(t - LAG_UPDATE)
-
-        @pl.when(t < chunks - 1)
-        def _():
-            begin(t + 1)
+            update_rest(t - LAG_UPDATE)
+
+        @pl.when((t >= LAG_CROSS) & (t < LAG_CROSS + chunks))
+        def _():
+            update_own(t - LAG_CROSS)
+
+        @pl.when(t < chunks - AHEAD)
+        def _():
+            begin(t + AHEAD)
+            message(CORE_SUM, cells, t + AHEAD).start()
 
         return carry
 
-    begin(0)
+    def early(q, carry):
+        begin(q)
+        return carry
+
+    lax.fori_loop(0, AHEAD, early, 0)
     pl.semaphore_wait(barrier, jnp.where(sends_halo, 5, 11))
     message(CORE_SUM, extra, 0).start()
+    for q in range(AHEAD):
+        message(CORE_SUM, cells, q).start()
     send_flux(0)
     lax.fori_loop(0, chunks + LAG_UPDATE, tick, 0)
 

time: 72.8 us -> 72.4 us (level)
  no operation moved by 1% of the time
where the time goes in v5:
time: 72.4 us; the launch traced here: 72.2 us
  Pallas kernels  70.6 us (98%)
  local copies, waits for them, and re-layouts  1.67 us (2%)
    pallas_call x1, Pallas kernels, body(): pl.pallas_call(functools.partial(kernel, depth, slabs), out_shape=pltpu.V...  70.6 us
    unnamed x1, local copies, waits for them, and re-layouts  1.67 us

profile of v5, /device:TPU:1, one launch (start us, length us, event | category | flops | bytes accessed | tf_op | source)
XLA Modules:
  0.0 72.2 jit_solution(13293710503653353642)
XLA Ops:
  0.0 70.6 %boltzmann_steps.1 = bf16[256,6,8,128]{3,2,1,0:T(8,128)(2,1)S(1)} custom-call(bf16[256,6,8,128]{3,2,1,0:T(8,128)(2,1)} %dist_ref.1, bf16[256,256]{1,0:T(8,128)(2,1)} %up_ref.1, bf16[256,256]{1,0:T(8,128)(2,1)} %down_ref.1, f32[2,128]{1,0:T(2,128)} %bitcast.1, s32[2,8,128]{2,1,0:T(8,128)} %wall_ref.1), custom_call_target="tpu_custom_call" | custom-call | flops 3221225472 | bytes 6291456 | tf_op jit(solution)/shard_map/boltzmann_steps/pallas_call | solution.py:529
  70.6 1.7 %copy.7 = bf16[256,6,8,128]{3,2,1,0:T(8,128)(2,1)} copy(bf16[256,6,8,128]{3,2,1,0:T(8,128)(2,1)S(1)} %boltzmann_steps.1) | data formatting | bytes 6291456

commit v6 on v5

--- a/solution.py
+++ b/solution.py
@@ -24,10 +24,11 @@
 
 CORE_SUM, PASS_SUM, NEAR_SUM, LAST_SUM, PAIR_SUM, OUT_B, OUT_A, OUT_PASS, CORE_OUT = range(9)
 LAG_FIRST, LAG_SECOND, LAG_THIRD, LAG_FINISH, LAG_PASS, LAG_CROSS, LAG_UPDATE = (
-    0, 2, 5, 8, 11, 13, 14,
+    0, 3, 7, 10, 13, 16, 17,
 )
-EDGE_TICK = 8
-AHEAD = 2
+EDGE_TICK = 7
+AHEAD = 3
+MIX_TICK = 14
 
 
 class Lane(NamedTuple):
@@ -414,22 +415,22 @@
             lax.fori_loop(0, 16, block, 0)
 
     order = [
-        (cross, LAG_CROSS),
-        (pass_on, LAG_PASS),
-        (finish_sums, LAG_FINISH),
-        (third_sums, LAG_THIRD),
-        (second_sums, LAG_SECOND),
-        (first_sums, LAG_FIRST),
+        (pass_on, LAG_PASS, 10),
+        (second_sums, LAG_SECOND, 3),
+        (first_sums, LAG_FIRST, 0),
+        (finish_sums, LAG_FINISH, 8),
+        (third_sums, LAG_THIRD, 6),
+        (cross, LAG_CROSS, 12),
     ]
 
     def tick(t, carry):
-        @pl.when(t == LAG_UPDATE)
+        @pl.when(t == MIX_TICK)
         def _():
             finish_mix()
 
-        for act, lag in order:
-
-            @pl.when(t == lag)
+        for act, lag, once in order:
+
+            @pl.when(t == once)
             def _(act=act):
                 act(extra, 0)
 

time: 72.4 us -> 72 us (level)
  no operation moved by 1% of the time
where the time goes in v6:
time: 72 us; the launch traced here: 71.8 us
  Pallas kernels  70.2 us (98%)
  local copies, waits for them, and re-layouts  1.67 us (2%)
    pallas_call x1, Pallas kernels, body(): pl.pallas_call(functools.partial(kernel, depth, slabs), out_shape=pltpu.V...  70.2 us
    unnamed x1, local copies, waits for them, and re-layouts  1.67 us

profile of v6, /device:TPU:1, one launch (start us, length us, event | category | flops | bytes accessed | tf_op | source)
XLA Modules:
  0.0 71.8 jit_solution(17760431436676234871)
XLA Ops:
  0.0 70.2 %boltzmann_steps.1 = bf16[256,6,8,128]{3,2,1,0:T(8,128)(2,1)S(1)} custom-call(bf16[256,6,8,128]{3,2,1,0:T(8,128)(2,1)} %dist_ref.1, bf16[256,256]{1,0:T(8,128)(2,1)} %up_ref.1, bf16[256,256]{1,0:T(8,128)(2,1)} %down_ref.1, f32[2,128]{1,0:T(2,128)} %bitcast.1, s32[2,8,128]{2,1,0:T(8,128)} %wall_ref.1), custom_call_target="tpu_custom_call" | custom-call | flops 3221225472 | bytes 6291456 | tf_op jit(solution)/shard_map/boltzmann_steps/pallas_call | solution.py:530
  70.2 1.7 %copy.7 = bf16[256,6,8,128]{3,2,1,0:T(8,128)(2,1)} copy(bf16[256,6,8,128]{3,2,1,0:T(8,128)(2,1)S(1)} %boltzmann_steps.1) | data formatting | bytes 6291456
